TPU v7x, 32 devices: a whole 2x2x4 slice. The times are simulated.
32 devices in a mesh: dp: 8 (over y, x, core), tensor: 4 (over z).
Axes of the slice: x: 2, y: 2, z: 4, core: 2. Of those that a mesh axis runs over, the one named last changes fastest.
Arguments:
- hidden: bfloat16 [4096, 4096], P('dp', 'tensor')
- w_query: bfloat16 [4096, 4096], P(None, 'tensor')
- w_key: bfloat16 [4096, 1024], P(None, 'tensor')
- w_value: bfloat16 [4096, 1024], P(None, 'tensor'), may hold values from -0.09375 to 0.09375
- w_out: bfloat16 [4096, 4096], P('tensor'), may hold values from -0.09375 to 0.09375
- doc_ids: int32 [4096], P('dp'), may hold values from 0 to 4095, as said below
- send_counts: int32 [8, 8], replicated, may hold values from 0 to 16, as said below
Outputs:
- attended: bfloat16 [5120, 4096], P('dp', 'tensor')
Inputs may be any that keep to these rules, and one draw needn't show every extreme that they name: `send_counts`: the diagonal is zero and each row sums to less than 512. On index i of dp the rows that stay come first, then the rows for each destination j in increasing order of j, each such block one whole document. `doc_ids`: the rows of one document lie together on one index of dp and share one id; different documents have different ids.
All inputs are finite; a program needn't handle non-finite values.
Results may differ from a plain program's by a relative error of at most 0.014.
Values may be sent and summed in bfloat16 or wider, within the bound.
A program may use at most 128 MiB of HBM per device.

v0:
```python
import jax
import jax.numpy as jnp
from jax import lax
from jax.sharding import PartitionSpec as P

HD = 128
SLOT = 16


def project_three(inputs, w_query, w_key, w_value):
    return tuple(
        (
            jnp.dot(inputs, weight, preferred_element_type=jnp.float32).astype(jnp.bfloat16)
            for weight in (w_query, w_key, w_value)
        )
    )


def project_slots(arrived, w_query, w_key, w_value):
    peers, slot_count = (arrived.shape[0], arrived.shape[1])
    flat = arrived.reshape(peers * slot_count, arrived.shape[2])
    return tuple(
        (
            result.reshape(peers, slot_count, -1)
            for result in project_three(flat, w_query, w_key, w_value)
        )
    )


def attend(queries, key_rows, value_rows, allowed, head_dim):
    batch, count = (queries.shape[0], queries.shape[1])
    kv_heads = key_rows.shape[2] // head_dim
    group = queries.shape[2] // key_rows.shape[2]
    query_part = queries.reshape(batch, count, kv_heads, group, head_dim)
    key_part = key_rows.reshape(batch, key_rows.shape[1], kv_heads, head_dim)
    value_part = value_rows.reshape(batch, value_rows.shape[1], kv_heads, head_dim)
    scores = jnp.einsum(
        "bqhgd,bkhd->bhgqk", query_part, key_part, preferred_element_type=jnp.float32
    ) * head_dim ** (-0.5)
    scores = jnp.where(allowed[:, None, None], scores, -jnp.inf)
    top = jnp.max(scores, axis=-1, keepdims=True)
    expo = jnp.exp(scores - top)
    total = jnp.sum(expo, axis=-1)
    mixed = jnp.einsum(
        "bhgqk,bkhd->bqhgd",
        expo.astype(jnp.bfloat16),
        value_part,
        preferred_element_type=jnp.float32,
    )
    mixed = mixed / jnp.transpose(total, (0, 3, 1, 2))[..., None]
    return mixed.reshape(batch, count, -1).astype(jnp.bfloat16)


def on_device(hidden, w_query, w_key, w_value, w_out, doc_ids, send_counts):
    peers = lax.axis_size("dp")
    my_index = lax.axis_index("dp")
    row_count = hidden.shape[0]
    head_dim = HD
    slot_count = SLOT
    home_full = lax.all_gather(hidden, "tensor", axis=1, tiled=True)
    home_q, home_k, home_v = project_three(home_full, w_query, w_key, w_value)
    outgoing = lax.dynamic_slice_in_dim(send_counts, my_index, 1, 0)[0]
    incoming = lax.dynamic_slice_in_dim(send_counts, my_index, 1, 1)[:, 0]
    home_len = row_count - jnp.sum(outgoing)
    block_start = home_len + jnp.cumsum(outgoing) - outgoing
    slot_ids = jnp.arange(slot_count, dtype=jnp.int32)
    peer_ids = jnp.arange(peers, dtype=jnp.int32)
    send_index = jnp.minimum(block_start[:, None] + slot_ids[None, :], row_count - 1).reshape(-1)
    send_valid = slot_ids[None, :] < outgoing[:, None]
    taken = jnp.take(home_full, send_index, axis=0).reshape(peers, slot_count, home_full.shape[1])
    moved = lax.all_to_all(
        jnp.where(send_valid[:, :, None], taken, jnp.zeros((), home_full.dtype)),
        "dp",
        split_axis=0,
        concat_axis=0,
        tiled=True,
    )
    recv_q, recv_k, recv_v = project_slots(moved, w_query, w_key, w_value)
    recv_valid = slot_ids[None, :] < incoming[:, None]
    home_pos = jnp.arange(row_count, dtype=jnp.int32)
    recv_labels = jnp.where(
        recv_valid,
        -1 - peer_ids[:, None],
        -1 - peers - peer_ids[:, None] * slot_count - slot_ids[None, :],
    )
    labels = jnp.concatenate([doc_ids, recv_labels.reshape(-1)])
    all_q = jnp.concatenate([home_q, recv_q.reshape(peers * slot_count, -1)], axis=0)
    all_k = jnp.concatenate([home_k, recv_k.reshape(peers * slot_count, -1)], axis=0)
    all_v = jnp.concatenate([home_v, recv_v.reshape(peers * slot_count, -1)], axis=0)
    positions = jnp.arange(labels.shape[0], dtype=jnp.int32)
    allowed = (labels[:, None] == labels[None, :]) & (positions[None, :] <= positions[:, None])
    mixed = attend(all_q[None], all_k[None], all_v[None], allowed[None], head_dim)[0]
    valid = jnp.concatenate([home_pos < home_len, recv_valid.reshape(-1)])
    partial_sum = jnp.dot(mixed, w_out, preferred_element_type=jnp.float32)
    partial_sum = jnp.where(valid[:, None], partial_sum, 0.0)
    return lax.psum_scatter(
        partial_sum.astype(jnp.bfloat16), "tensor", scatter_dimension=1, tiled=True
    )


def solution(mesh):
    in_specs = (
        P("dp", "tensor"),
        P(None, "tensor"),
        P(None, "tensor"),
        P(None, "tensor"),
        P("tensor", None),
        P("dp"),
        P(),
    )
    out_specs = P("dp", "tensor")
    return jax.shard_map(
        on_device, mesh=mesh, in_specs=in_specs, out_specs=out_specs, check_vma=False
    )
```

profile of v0, /device:TPU:0, one launch (start us, length us, event | category | flops | bytes accessed | tf_op | source)
XLA Modules:
  0.0 261.8 jit_solution(16791029091151933763)
XLA Ops:
  6.5 0.7 all-gather.2.cloned.1.call-update
  7.3 0.9 dynamic-slice_reduce_fusion
  8.1 0.1 iota_compare_fusion.2
  8.2 0.1 lt.82
  8.3 1.3 fusion.17
  9.6 0.2 reduce-window.8
  10.6 0.1 min.22
  10.7 0.1 sub.55
  10.9 0.1 broadcast_in_dim.77
  11.0 0.7 pad_add_fusion
  11.8 1.1 fusion.10
  12.9 79.6 %all-gather.2.cloned.1.call-done = bf16[512,4096]{1,0:T(8,128)(2,1)} async-done(((bf16[512,1024]{1,0:T(8,128)(2,1)}), bf16[512,4096]{1,0:T(8,128)(2,1)}) %all-gather.2.cloned.1.call-update) | async-done | bytes 4194320 | tf_op jit(solution)/shard_map/all_gather | solution.py:60
  92.4 4.9 %gather_fusion = bf16[128,4096]{1,0:T(8,128)(2,1)S(1)} fusion(bf16[512,4096]{1,0:T(8,128)(2,1)} %all-gather.2.cloned.1.call-done, s32[1024]{0:T(1024)S(1)} %pad_clamp_fusion), kind=kCustom, calls=%fused_computation | custom fusion | bytes 2097664 | tf_op jit(solution)/shard_map/jit(_take)/gather | solution.py:70
  97.4 1.2 select_select_fusion
  98.6 3.7 %all-to-all-start = ((bf16[8,16,4096]{2,1,0:T(8,128)(2,1)}), bf16[8,16,4096]{2,1,0:T(8,128)(2,1)S(1)}, u32[]{:S(2)}, u32[]{:S(2)}) async-start(bf16[8,16,4096]{2,1,0:T(8,128)(2,1)} %select_select_fusion), calls=%async_computation | async-start | bytes 2097152 | tf_op jit(solution)/shard_map/all_to_all | solution.py:71
  102.3 10.3 %convolution_convert_fusion = bf16[512,1024]{1,0:T(8,128)(2,1)} fusion(bf16[512,4096]{1,0:T(8,128)(2,1)} %all-gather.2.cloned.1.call-done, bf16[4096,1024]{1,0:T(8,128)(2,1)} %param.8), kind=kOutput, calls=%fused_computation.14 | convolution fusion | flops 4295491584 | bytes 13631488 | tf_op jit(solution)/shard_map/dot_general | solution.py:13
  112.5 2.0 convolution_convert_fusion.2
  114.5 2.0 convolution_convert_fusion.3
  116.4 1.2 all-to-all-done
  117.6 0.4 convolution_convert_fusion.4
  118.1 2.0 convolution_convert_fusion.5
  120.1 5.4 %convolution_convert_fusion.1 = bf16[128,1024]{1,0:T(8,128)(2,1)} fusion(bf16[128,4096]{1,0:T(8,128)(2,1)S(1)} %bitcast.64, bf16[4096,1024]{1,0:T(8,128)(2,1)} %param.8), kind=kOutput, calls=%fused_computation.18 | convolution fusion | flops 1073872896 | bytes 9699328 | tf_op jit(solution)/shard_map/dot_general | solution.py:13
  125.5 0.8 reshape.209
  126.3 1.4 pad_maximum_fusion
  127.8 2.0 reshape.210
  129.7 1.0 pad_maximum_fusion.1
  130.7 0.2 copy.15
  130.9 8.5 %fusion.2 = (f32[2,4,640]{2,1,0:T(4,128)S(1)}, f32[2,640,640,4]{2,1,3,0:T(8,128)}) fusion(pred[640,640]{0,1:T(8,128)(4,1)} %fusion.10, bf16[640,2,4,128]{3,2,1,0:T(4,128)(2,1)} %reshape.210, bf16[640,2,128,1]{2,1,0,3:T(2,128)(2,1)} %bitcast.66), kind=kOutput, calls=%fused_computation.6 | convolution fusion | flops 848686080 | bytes 15175680 | tf_op jit(solution)/shard_map/bqhgd,bkhd->bhgqk/dot_general | solution.py:37
  139.4 7.6 %fusion = f32[2,4,640]{2,1,0:T(4,128)S(1)} fusion(f32[2,640,640,4]{2,1,3,0:T(8,128)} %get-tuple-element.8, f32[2,4,640]{2,1,0:T(4,128)S(1)} %get-tuple-element.7, pred[640,640]{0,1:T(8,128)(4,1)S(1)} %copy-done.3), kind=kLoop, calls=%fused_computation.3 | loop fusion | flops 13102080 | bytes 13557760 | tf_op jit(solution)/shard_map/reduce_sum | solution.py:43
  147.0 8.6 %fusion.7 = bf16[1,640,2,4,128]{1,4,3,2,0:T(8,128)(2,1)S(1)} fusion(bf16[640,2,128,1]{0,2,3,1:T(8,128)(2,1)S(1)} %bitcast.67, f32[2,640,640,4]{2,1,3,0:T(8,128)} %get-tuple-element.8, f32[2,4,640]{2,1,0:T(4,128)S(1)} %get-tuple-element.7, pred[640,640]{0,1:T(8,128)(4,1)S(1)} %copy-done.3, f32[640,2,4]{0,2,1:T(4,128)S(1)} %bitcast.68), kind=kOutput, calls=%fused_computation.11 | convolution fusion | flops 853278720 | bytes 15196160 | tf_op jit(solution)/shard_map/bhgqk,bkhd->bqhgd/dot_general | solution.py:44
  155.6 7.6 %select_convert_fusion = bf16[640,4096]{1,0:T(8,128)(2,1)} fusion(bf16[640,1024]{0,1:T(8,128)(2,1)S(1)} %bitcast.73, bf16[1024,4096]{1,0:T(8,128)(2,1)S(1)} %bitcast.72, pred[640]{0:T(1024)(128)(4,1)S(1)} %pad_add_fusion.1), kind=kOutput, calls=%fused_computation.5 | convolution fusion | flops 5373952000 | bytes 14942848 | tf_op jit(solution)/shard_map/dot_general | solution.py:94
  163.2 91.8 %reduce-scatter.2.cloned.1.call-done = bf16[640,1024]{1,0:T(8,128)(2,1)} async-done(((bf16[640,4096]{1,0:T(8,128)(2,1)}), bf16[640,1024]{1,0:T(8,128)(2,1)}) %reduce-scatter.2.cloned.1.call-update) | async-done | bytes 1310736 | tf_op jit(solution)/shard_map/reduce_scatter | solution.py:96
  (31 shorter events, 0.5 us)
Async XLA Ops:
  6.5 106.0 %copy-start = (bf16[4096,256]{1,0:T(8,128)(2,1)S(1)}, bf16[4096,256]{1,0:T(8,128)(2,1)}, u32[]{:S(2)}) copy-start(bf16[4096,256]{1,0:T(8,128)(2,1)} %param.9) | copy-start | bytes 6291460
  6.5 85.9 %all-gather.2.cloned.1.call-start = ((), (), s32[]{:S(2)}) async-start(), calls=%async_computation.2 | async-start | bytes 5242880 | tf_op jit(solution)/shard_map/all_gather | solution.py:60
  98.6 19.1 %all-to-all-start = ((bf16[8,16,4096]{2,1,0:T(8,128)(2,1)}), bf16[8,16,4096]{2,1,0:T(8,128)(2,1)S(1)}, u32[]{:S(2)}, u32[]{:S(2)}) async-start(bf16[8,16,4096]{2,1,0:T(8,128)(2,1)} %select_select_fusion), calls=%async_computation | async-start | bytes 2097152 | tf_op jit(solution)/shard_map/all_to_all | solution.py:71
  102.2 152.8 %reduce-scatter.2.cloned.1.call-start = ((), (), s32[]{:S(2)}) async-start(), calls=%async_computation.3 | async-start | bytes 6553600 | tf_op jit(solution)/shard_map/reduce_scatter | solution.py:96
  102.3 10.3 %copy-start.1 = (bf16[512,4096]{1,0:T(8,128)(2,1)S(1)}, bf16[512,4096]{1,0:T(8,128)(2,1)}, u32[]{:S(2)}) copy-start(bf16[512,4096]{1,0:T(8,128)(2,1)} %all-gather.2.cloned.1.call-done) | copy-start | bytes 12582916
  112.5 2.0 copy-start.2
  120.1 5.4 %copy-start.4 = (bf16[512,256]{1,0:T(8,128)(2,1)S(1)}, bf16[512,256]{1,0:T(8,128)(2,1)}, u32[]{:S(2)}) copy-start(bf16[512,256]{1,0:T(8,128)(2,1)} %convolution_convert_fusion.2) | copy-start | bytes 786436
  130.9 8.5 %copy-start.3 = (pred[640,640]{0,1:T(8,128)(4,1)S(1)}, pred[640,640]{0,1:T(8,128)(4,1)}, u32[]{:S(2)}) copy-start(pred[640,640]{0,1:T(8,128)(4,1)} %fusion.10) | copy-start | bytes 1228804
  139.4 16.2 %slice-start = ((s8[8388608]{0:T(1024)(128)(4,1)}), s8[4194304]{0:T(1024)(128)(4,1)S(1)}, s32[]{:S(2)}) async-start(s8[8388608]{0:T(1024)(128)(4,1)} %bitcast.71), calls=%async_computation.4 | async-start | bytes 8388608
  147.0 8.6 %slice-start.1 = ((s8[8388608]{0:T(1024)(128)(4,1)}), s8[4194304]{0:T(1024)(128)(4,1)S(1)}, s32[]{:S(2)}) async-start(s8[8388608]{0:T(1024)(128)(4,1)} %bitcast.71), calls=%async_computation.5 | async-start | bytes 8388608
Sparse Core Ops, SparseCore 0:
  8.9 83.4 all-gather.1
  163.4 91.5 reduce-scatter.1
where the time goes:
time: 262 us
  waiting for transfers between devices  173 us (66%)
  matrix products  46.7 us (18%)
  other arithmetic  14.8 us (6%)
  between operations  14.2 us (5%)
  local copies, waits for them, and re-layouts  9.22 us (4%)
  starting transfers between devices  3.69 us (1%)
    reduce_scatter x1, waiting for transfers between devices, on_device(): lax.psum_scatter(partial_sum.astype(jnp.bfloat16), 'tensor', scatter_dime...  91.8 us
    all_gather x1, waiting for transfers between devices, on_device(): home_full = lax.all_gather(hidden, 'tensor', axis=1, tiled=True)  79.6 us
    dot_general x6, matrix products, project_three(): jnp.dot(inputs, weight, preferred_element_type=jnp.float32)  22 us
    dot_general x1, matrix products, attend(): jnp.einsum('bhgqk,bkhd->bqhgd', expo.astype(jnp.bfloat16), value_part, pr...  8.6 us
    dot_general x1, matrix products, attend(): jnp.einsum('bqhgd,bkhd->bhgqk', query_part, key_part, preferred_element_t...  8.48 us
    dot_general x1, matrix products, on_device(): partial_sum = jnp.dot(mixed, w_out, preferred_element_type=jnp.float32)  7.6 us
    reduce_sum x1, other arithmetic, attend(): total = jnp.sum(expo, axis=-1)  7.56 us
  transfers between devices with their start and end apart: 3, of which 3 were waited for; matrix products, arithmetic and copies ran while one was open for 7% of the time, Pallas kernels for 0%

commit v1 on v0

v1 whole, which is shorter than its diff:
```python
import functools

import jax
import jax.numpy as jnp
from jax import lax
from jax.experimental import pallas as pl
from jax.experimental.pallas import tpu as pltpu
from jax.sharding import PartitionSpec as P

HD = 128
SLOT = 16
TILE = 256
CHUNKS = 4
MESH = pl.DeviceIdType.MESH
F32 = jnp.float32
BF16 = jnp.bfloat16


def layer_kernel(
    peers, parts, chunks, q_heads, kv_heads,
    hidden_ref, wq_ref, wk_ref, wv_ref, wo_ref, docs_ref, counts_ref,
    out_ref,
    wqkv, wout, hid, heads, mixed, partial, arrived, acc, final, outgoing, slots, doc_col,
    load_sem, ag_send, ag_recv, rs_send, rs_recv, mv_send, mv_recv,
):
    rows_all, width = hidden_ref.shape
    count = rows_all // chunks
    group = q_heads // kv_heads
    me = lax.axis_index("dp")
    z = lax.axis_index("tensor")
    tiles_per_block = width // TILE

    def inside(position):
        return (position >= 0) & (position < parts)

    def clamp(position):
        return jnp.minimum(jnp.maximum(position, 0), parts - 1)

    q_cols, kv_cols = q_heads * HD, kv_heads * HD
    load_own = pltpu.make_async_copy(hidden_ref, hid.at[z], load_sem.at[0])
    loads_qkv = [
        pltpu.make_async_copy(wq_ref, wqkv.at[:, pl.ds(0, q_cols)], load_sem.at[1]),
        pltpu.make_async_copy(wk_ref, wqkv.at[:, pl.ds(q_cols, kv_cols)], load_sem.at[2]),
        pltpu.make_async_copy(wv_ref, wqkv.at[:, pl.ds(q_cols + kv_cols, kv_cols)], load_sem.at[3]),
    ]
    load_out = pltpu.make_async_copy(wo_ref, wout, load_sem.at[4])

    barrier = pltpu.get_barrier_semaphore()
    for step in (-1, 1):
        @pl.when(inside(z + step))
        def _(step=step):
            pl.semaphore_signal(barrier, inc=1, device_id={"tensor": z + step}, device_id_type=MESH)

    @pl.loop(1, peers)
    def _(i):
        pl.semaphore_signal(barrier, inc=1, device_id={"dp": lax.rem(me + i, peers)}, device_id_type=MESH)

    load_own.start()
    for load in loads_qkv:
        load.start()
    load_out.start()
    neighbours = inside(z - 1).astype(jnp.int32) + inside(z + 1).astype(jnp.int32)
    pl.semaphore_wait(barrier, peers - 1 + neighbours)

    def rows_of(c):
        return pl.ds(c * count, count)

    def gather_copy(way, c, hop):
        step = 1 - 2 * way
        owner = clamp(z - step * (hop - 1))
        block = hid.at[owner, rows_of(c), :]
        return pltpu.make_async_remote_copy(
            src_ref=hidden_ref.at[rows_of(c), :] if hop == 1 else block,
            dst_ref=block,
            send_sem=ag_send.at[way, c, hop - 1],
            recv_sem=ag_recv.at[way, c, hop - 1],
            device_id={"tensor": clamp(z + step)},
            device_id_type=MESH,
        )

    def gather_sends(way, hop):
        step = 1 - 2 * way
        return inside(z - step * (hop - 1)) & inside(z + step)

    def gather_start(c, hop):
        for way in (0, 1):
            @pl.when(gather_sends(way, hop))
            def _(way=way):
                gather_copy(way, c, hop).start()

    def gather_take(c, hop):
        for way in (0, 1):
            step = 1 - 2 * way

            @pl.when(inside(z - step * hop))
            def _(way=way, step=step):
                block = hid.at[clamp(z - step * hop), rows_of(c), :]
                pltpu.make_async_remote_copy(
                    src_ref=block,
                    dst_ref=block,
                    send_sem=ag_send.at[way, c, hop - 1],
                    recv_sem=ag_recv.at[way, c, hop - 1],
                    device_id={"tensor": clamp(z + step)},
                    device_id_type=MESH,
                ).wait_recv()
        if hop < parts - 1:
            gather_start(c, hop + 1)

    def sum_copy(way, c, hop, source):
        step = 1 - 2 * way
        return pltpu.make_async_remote_copy(
            src_ref=source,
            dst_ref=arrived.at[way, c, hop - 1],
            send_sem=rs_send.at[way, c, hop - 1],
            recv_sem=rs_recv.at[way, c, hop - 1],
            device_id={"tensor": clamp(z + step)},
            device_id_type=MESH,
        )

    def sum_hop(c, hop):
        for way in (0, 1):
            step = 1 - 2 * way
            block = z + step * (parts - hop)
            first = jnp.logical_not(inside(z - step))

            @pl.when(inside(block) & first)
            def _(way=way, block=block):
                sum_copy(way, c, hop, partial.at[c, clamp(block)]).start()

            if hop > 1:
                @pl.when(inside(block) & jnp.logical_not(first))
                def _(way=way, block=block):
                    slot = arrived.at[way, c, hop - 2]
                    sum_copy(way, c, hop - 1, slot).wait_recv()
                    slot[...] = (slot[...].astype(F32) + partial[c, clamp(block)].astype(F32)).astype(BF16)
                    sum_copy(way, c, hop, slot).start()

    own_counts = counts_ref[pl.ds(me, 1), :].astype(F32)
    home_len = rows_all - jnp.sum(own_counts, axis=1, keepdims=True)

    def sum_finish(c):
        acc[...] = partial[c, z].astype(F32)
        for way in (0, 1):
            step = 1 - 2 * way

            @pl.when(inside(z - step))
            def _(way=way):
                slot = arrived.at[way, c, parts - 2]
                sum_copy(way, c, parts - 1, slot).wait_recv()
                acc[...] += slot[...].astype(F32)
        total = acc[...]
        final[rows_of(c), :] = total.astype(BF16)
        position = (lax.broadcasted_iota(jnp.int32, (count, 1), 0) + c * count).astype(F32)
        out_ref[rows_of(c), :] = jnp.where(position < home_len, total, 0.0).astype(BF16)

    def project(c):
        @pl.loop(0, wqkv.shape[1] // TILE)
        def _(i):
            columns = pl.ds(pl.multiple_of(i * TILE, TILE), TILE)
            total = jnp.zeros((count, TILE), F32)
            for b in range(parts):
                total += jnp.dot(
                    hid[b, rows_of(c), :],
                    wqkv[pl.ds(b * width, width), columns],
                    preferred_element_type=F32,
                )
            rounded = total.astype(BF16)
            for k in range(TILE // HD):
                heads[i * (TILE // HD) + k, rows_of(c), :] = rounded[:, k * HD:(k + 1) * HD]

    doc_row = docs_ref[...].astype(F32)

    def attend(c):
        seen = (c + 1) * count
        seen_rows = pl.ds(0, seen)
        query_at = lax.broadcasted_iota(jnp.int32, (count, seen), 0) + c * count
        key_at = lax.broadcasted_iota(jnp.int32, (count, seen), 1)
        same = doc_col[rows_of(c), :][:, :1] == doc_row[:, :seen]
        allowed = same & (key_at <= query_at)

        @pl.loop(0, kv_heads)
        def _(g):
            keys = heads[q_heads + g, seen_rows, :]
            values = heads[q_heads + kv_heads + g, seen_rows, :]
            for k in range(group):
                query = heads[g * group + k, rows_of(c), :]
                scores = lax.dot_general(
                    query, keys, (((1,), (1,)), ((), ())), preferred_element_type=F32
                ) * HD ** (-0.5)
                scores = jnp.where(allowed, scores, -jnp.inf)
                expo = jnp.exp(scores - jnp.max(scores, axis=1, keepdims=True))
                total = jnp.sum(expo, axis=1, keepdims=True)
                mix = jnp.dot(expo.astype(BF16), values, preferred_element_type=F32) / total
                columns = pl.ds(pl.multiple_of((g * group + k) * HD, HD), HD)
                mixed[:, columns] = mix.astype(BF16)

    def project_out(c):
        @pl.loop(0, parts * tiles_per_block)
        def _(i):
            columns = pl.ds(pl.multiple_of(i * TILE, TILE), TILE)
            total = jnp.dot(mixed[...], wout[:, columns], preferred_element_type=F32)
            inner = pl.ds(pl.multiple_of(lax.rem(i, tiles_per_block) * TILE, TILE), TILE)
            partial[c, lax.div(i, tiles_per_block), :, inner] = total.astype(BF16)

    gather_start(0, 1)
    for k in range(rows_all // HD):
        doc_col[pl.ds(k * HD, HD), :] = jnp.broadcast_to(doc_row[:, k * HD:(k + 1) * HD], (HD, HD)).T
    for hop in range(1, parts - 1):
        gather_take(0, hop)
    if chunks > 1:
        gather_start(1, 1)
    load_own.wait()
    for c in range(chunks):
        gather_take(c, parts - 1)
        if c == 0:
            for load in loads_qkv:
                load.wait()
        project(c)
        if c + 1 < chunks:
            for hop in range(1, parts - 2):
                gather_take(c + 1, hop)
        if c > 0:
            for hop in range(2, parts - 1):
                sum_hop(c - 1, hop)
        attend(c)
        if c == 0:
            load_out.wait()
        project_out(c)
        if c + 1 < chunks:
            gather_take(c + 1, parts - 2)
            if c + 2 < chunks:
                gather_start(c + 2, 1)
        if c > 0:
            sum_hop(c - 1, parts - 1)
        sum_hop(c, 1)
        if c > 0:
            sum_finish(c - 1)
    for hop in range(2, parts):
        sum_hop(chunks - 1, hop)
    sum_finish(chunks - 1)

    moved = peers * SLOT
    at = lax.broadcasted_iota(jnp.int32, (moved, peers), 0)
    to = lax.broadcasted_iota(jnp.int32, (moved, peers), 1)
    goal = lax.div(at, SLOT)
    counts = jnp.broadcast_to(own_counts, (moved, peers))
    length = jnp.sum(jnp.where(to == goal, counts, 0.0), axis=1, keepdims=True)
    before = jnp.sum(jnp.where(to < goal, counts, 0.0), axis=1, keepdims=True)
    place = lax.rem(lax.broadcasted_iota(jnp.int32, (moved, 1), 0), SLOT).astype(F32)
    index = jnp.where(place < length, home_len + before + place, -1.0)
    lanes = lax.broadcasted_iota(jnp.int32, (moved, rows_all), 1).astype(F32)
    pick = jnp.where(index == lanes, 1.0, 0.0).astype(BF16)
    outgoing[...] = jnp.dot(pick, final[...], preferred_element_type=F32).astype(BF16)

    def move_copy(i, goal, place):
        return pltpu.make_async_remote_copy(
            src_ref=outgoing.at[pl.ds(pl.multiple_of(goal * SLOT, SLOT), SLOT), :],
            dst_ref=slots.at[pl.ds(pl.multiple_of(place * SLOT, SLOT), SLOT), :],
            send_sem=mv_send.at[i - 1],
            recv_sem=mv_recv.at[i - 1],
            device_id={"dp": goal},
            device_id_type=MESH,
        )

    @pl.loop(1, peers)
    def _(i):
        move_copy(i, lax.rem(me + i, peers), me).start()

    slots[pl.ds(pl.multiple_of(me * SLOT, SLOT), SLOT), :] = outgoing[
        pl.ds(pl.multiple_of(me * SLOT, SLOT), SLOT), :
    ]

    for way in (0, 1):
        for hop in range(1, parts):
            @pl.when(gather_sends(way, hop))
            def _(way=way, hop=hop):
                for c in range(chunks):
                    gather_copy(way, c, hop).wait_send()

            @pl.when(inside(z + (1 - 2 * way) * (parts - hop)))
            def _(way=way, hop=hop):
                for c in range(chunks):
                    sum_copy(way, c, hop, arrived.at[way, c, hop - 1]).wait_send()

    @pl.loop(1, peers)
    def _(i):
        move_copy(i, lax.rem(me + i, peers), lax.rem(me + peers - i, peers)).wait()

    out_ref[pl.ds(rows_all, moved), :] = slots[...]


def on_device(hidden, w_query, w_key, w_value, w_out, doc_ids, send_counts):
    peers = lax.axis_size("dp")
    parts = lax.axis_size("tensor")
    rows, width = hidden.shape
    q_heads = w_query.shape[1] // HD
    kv_heads = w_key.shape[1] // HD
    chunks = CHUNKS
    count = rows // chunks
    features = w_query.shape[0]
    moved = peers * SLOT
    anywhere = pl.BlockSpec(memory_space=pl.ANY)
    in_vmem = pl.BlockSpec(memory_space=pltpu.VMEM)
    hops = parts - 1
    return pl.pallas_call(
        functools.partial(layer_kernel, peers, parts, chunks, q_heads, kv_heads),
        out_shape=jax.ShapeDtypeStruct((rows + moved, width), BF16),
        in_specs=[anywhere] * 5 + [in_vmem] * 2,
        out_specs=in_vmem,
        scratch_shapes=[
            pltpu.VMEM((features, (q_heads + 2 * kv_heads) * HD), BF16),
            pltpu.VMEM(w_out.shape, BF16),
            pltpu.VMEM((parts, rows, width), BF16),
            pltpu.VMEM((q_heads + 2 * kv_heads, rows, HD), BF16),
            pltpu.VMEM((count, q_heads * HD), BF16),
            pltpu.VMEM((chunks, parts, count, width), BF16),
            pltpu.VMEM((2, chunks, hops, count, width), BF16),
            pltpu.VMEM((count, width), F32),
            pltpu.VMEM((rows, width), BF16),
            pltpu.VMEM((moved, width), BF16),
            pltpu.VMEM((moved, width), BF16),
            pltpu.VMEM((rows, HD), F32),
            pltpu.SemaphoreType.DMA((5,)),
            pltpu.SemaphoreType.DMA((2, chunks, hops)),
            pltpu.SemaphoreType.DMA((2, chunks, hops)),
            pltpu.SemaphoreType.DMA((2, chunks, hops)),
            pltpu.SemaphoreType.DMA((2, chunks, hops)),
            pltpu.SemaphoreType.DMA((peers - 1,)),
            pltpu.SemaphoreType.DMA((peers - 1,)),
        ],
        compiler_params=pltpu.CompilerParams(
            collective_id=0, has_side_effects=True, vmem_limit_bytes=58 * 1024 * 1024
        ),
        name="layer",
    )(hidden, w_query, w_key, w_value, w_out, doc_ids.reshape(1, rows), send_counts)


def solution(mesh):
    in_specs = (
        P("dp", "tensor"),
        P(None, "tensor"),
        P(None, "tensor"),
        P(None, "tensor"),
        P("tensor", None),
        P("dp"),
        P(),
    )
    return jax.shard_map(
        on_device, mesh=mesh, in_specs=in_specs, out_specs=P("dp", "tensor"), check_vma=False
    )
```

time: 262 us -> 134 us (0.51)
  waiting for transfers between devices: 173 us -> 0 us
  Pallas kernels: 0 us -> 131 us
  matrix products: 46.7 us -> 0 us
  other arithmetic: 14.8 us -> 0 us
  between operations: 14.2 us -> 0.01 us
  local copies, waits for them, and re-layouts: 9.22 us -> 2.47 us
  starting transfers between devices: 3.69 us -> 0 us
    pallas_call x0 -> x1, Pallas kernels: none -> 131 us  [on_device(): pl.pallas_call(functools.partial(layer_kernel, peers, parts, chunks, q_he...]
    reduce_scatter x1 -> x0, waiting for transfers between devices: 91.8 us -> none  [on_device(): lax.psum_scatter(partial_sum.astype(jnp.bfloat16), 'tensor', scatter_dime...]
    all_gather x1 -> x0, waiting for transfers between devices: 79.6 us -> none  [on_device(): home_full = lax.all_gather(hidden, 'tensor', axis=1, tiled=True)]
    dot_general x9 -> x0, matrix products: 46.7 us -> none  [the longest x6 22 us: project_three(): jnp.dot(inputs, weight, preferred_element_type=jnp.float32)]
    reduce_sum x2 -> x0, other arithmetic: 8.89 us -> none  [the longest x1 7.56 us: attend(): total = jnp.sum(expo, axis=-1)]
    gather x1 -> x0, local copies, waits for them, and re-layouts: 4.93 us -> none  [on_device(): jnp.take(home_full, send_index, axis=0)]
    all_to_all x1 -> x0, starting transfers between devices: 3.65 us -> none  [on_device(): lax.all_to_all(jnp.where(send_valid[:, :, None], taken, jnp.zeros((), hom...]
    concatenate x5 -> x0, other arithmetic: 3.1 us -> none  [the longest x1 1.41 us: on_device(): jnp.concatenate([home_q, recv_q.reshape(peers * slot_count, -1)], axis=0)]
  transfers between devices with their start and end apart: 3 -> 0, of which waited for: 3 -> 0; matrix products, arithmetic and copies ran while one was open for 7% -> 0% of each run, Pallas kernels for 0% -> 0%
where the time goes in v1:
time: 134 us
  Pallas kernels  131 us (98%)
  local copies, waits for them, and re-layouts  2.47 us (2%)
    pallas_call x1, Pallas kernels, on_device(): pl.pallas_call(functools.partial(layer_kernel, peers, parts, chunks, q_he...  131 us

profile of v1, /device:TPU:0, one launch (start us, length us, event | category | flops | bytes accessed | tf_op | source)
XLA Modules:
  0.0 133.5 jit_solution(9973563307034548696)
XLA Ops:
  0.0 131.0 %layer.1 = bf16[640,1024]{1,0:T(8,128)(2,1)} custom-call(bf16[512,1024]{1,0:T(8,128)(2,1)} %hidden_ref.1, bf16[4096,1024]{1,0:T(8,128)(2,1)} %wq_ref.1, bf16[4096,256]{1,0:T(8,128)(2,1)} %wk_ref.1, bf16[4096,256]{1,0:T(8,128)(2,1)} %wv_ref.1, bf16[1024,4096]{1,0:T(8,128)(2,1)} %wo_ref.1, s32[1,512]{1,0:T(1,128)} %bitcast.1, s32[8,8]{1,0:T(8,128)} %counts_ref.1), custom_call_target="tpu_custom_call" | custom-call | tf_op jit(solution)/shard_map/layer/pallas_call | solution.py:305
  131.0 2.5 %copy.9 = bf16[640,1024]{1,0:T(8,128)(2,1)} copy(bf16[640,1024]{1,0:T(8,128)(2,1)} %layer.1) | data formatting | bytes 2621440

commit v2 on v1

--- a/solution.py
+++ b/solution.py
@@ -10,21 +10,78 @@
 HD = 128
 SLOT = 16
 TILE = 256
-CHUNKS = 4
 MESH = pl.DeviceIdType.MESH
 F32 = jnp.float32
 BF16 = jnp.bfloat16
+SIZES = (64, 64, 128, 128, 64, 64)
+ORDER = (
+    ("send", 0), ("send", 1), ("take", 0, 1, 0), ("take", 0, 1, 1), ("send", 2), ("take", 0, 2, 0),
+    ("take", 0, 3, 0), ("take", 0, 2, 1), ("take", 0, 3, 1), ("project", 0, 0), ("project", 0, 1),
+    ("take", 1, 1, 0), ("attend", 0), ("take", 1, 1, 1), ("take", 1, 2, 1), ("out", 0, 0), ("out", 0, 1),
+    ("take", 1, 2, 0), ("take", 1, 3, 0), ("send", 3), ("sum", 0, 1, 0), ("sum", 0, 1, 1), ("take", 1, 3, 1),
+    ("project", 1, 0), ("project", 1, 1), ("attend", 1), ("out", 1, 0), ("out", 1, 1), ("take", 2, 1, 1),
+    ("sum", 1, 1, 1), ("sum", 1, 1, 0), ("take", 2, 1, 0), ("take", 2, 2, 1), ("take", 2, 2, 0), ("take", 3, 1, 0),
+    ("sum", 0, 2, 1), ("take", 3, 1, 1), ("sum", 1, 2, 0), ("sum", 0, 2, 0), ("send", 5), ("take", 2, 3, 1),
+    ("send", 4), ("sum", 1, 3, 0), ("take", 2, 3, 0), ("sum", 1, 2, 1), ("project", 2, 0), ("project", 2, 1),
+    ("attend", 2), ("take", 3, 2, 1), ("take", 3, 2, 0), ("sum", 0, 3, 1), ("out", 2, 0), ("out", 2, 1),
+    ("sum", 2, 1, 1), ("sum", 2, 2, 1), ("sum", 2, 1, 0), ("take", 4, 1, 0), ("take", 5, 1, 0), ("take", 4, 1, 1),
+    ("take", 5, 1, 1), ("sum", 2, 2, 0), ("sum", 2, 3, 1), ("take", 3, 3, 1), ("sum", 2, 3, 0), ("take", 3, 3, 0),
+    ("project", 3, 0), ("project", 3, 1), ("take", 4, 2, 0), ("take", 4, 2, 1), ("sum", 0, 3, 0), ("sum", 1, 3, 1),
+    ("attend", 3), ("out", 3, 0), ("out", 3, 1), ("sum", 3, 1, 1), ("take", 5, 2, 0), ("sum", 3, 2, 1),
+    ("sum", 3, 1, 0), ("take", 4, 3, 0), ("sum", 3, 2, 0), ("take", 5, 2, 1), ("take", 4, 3, 1), ("project", 4, 0),
+    ("project", 4, 1), ("attend", 4), ("out", 4, 0), ("out", 4, 1), ("sum", 3, 3, 0), ("sum", 4, 1, 1),
+    ("take", 5, 3, 0), ("take", 5, 3, 1), ("sum", 3, 3, 1), ("project", 5, 0), ("project", 5, 1), ("attend", 5),
+    ("sum", 4, 1, 0), ("out", 5, 0), ("out", 5, 1), ("sum", 5, 1, 0), ("finish", 0), ("sum", 4, 2, 0),
+    ("sum", 5, 1, 1), ("sum", 4, 2, 1), ("sum", 5, 2, 0), ("sum", 5, 2, 1), ("finish", 2), ("sum", 4, 3, 1),
+    ("finish", 1), ("sum", 4, 3, 0), ("sum", 5, 3, 1), ("sum", 5, 3, 0), ("finish", 4), ("finish", 3),
+    ("finish", 5),
+)
+
+
+def plain_order(parts, chunks):
+    last = parts - 1
+    order = [("send", 0)]
+
+    def both(kind, c, hops):
+        for hop in hops:
+            for way in (0, 1):
+                order.append((kind, c, hop, way))
+
+    both("take", 0, range(1, last))
+    if chunks > 1:
+        order.append(("send", 1))
+    for c in range(chunks):
+        both("take", c, (last,))
+        order.extend([("project", c, 0), ("project", c, 1)])
+        if c + 1 < chunks:
+            both("take", c + 1, range(1, last - 1))
+        if c > 0:
+            both("sum", c - 1, range(2, last))
+        order.extend([("attend", c), ("out", c, 0), ("out", c, 1)])
+        if c + 1 < chunks:
+            both("take", c + 1, (last - 1,))
+            if c + 2 < chunks:
+                order.append(("send", c + 2))
+        if c > 0:
+            both("sum", c - 1, (last,))
+        both("sum", c, (1,))
+        if c > 0:
+            order.append(("finish", c - 1))
+    both("sum", chunks - 1, range(2, parts))
+    order.append(("finish", chunks - 1))
+    return order
 
 
 def layer_kernel(
-    peers, parts, chunks, q_heads, kv_heads,
+    peers, parts, sizes, order, q_heads, kv_heads,
     hidden_ref, wq_ref, wk_ref, wv_ref, wo_ref, docs_ref, counts_ref,
     out_ref,
     wqkv, wout, hid, heads, mixed, partial, arrived, acc, final, outgoing, slots, doc_col,
     load_sem, ag_send, ag_recv, rs_send, rs_recv, mv_send, mv_recv,
 ):
     rows_all, width = hidden_ref.shape
-    count = rows_all // chunks
+    chunks = len(sizes)
+    starts = [sum(sizes[:c]) for c in range(chunks)]
     group = q_heads // kv_heads
     me = lax.axis_index("dp")
     z = lax.axis_index("tensor")
@@ -63,7 +120,7 @@
     pl.semaphore_wait(barrier, peers - 1 + neighbours)
 
     def rows_of(c):
-        return pl.ds(c * count, count)
+        return pl.ds(starts[c], sizes[c])
 
     def gather_copy(way, c, hop):
         step = 1 - 2 * way
@@ -82,79 +139,88 @@
         step = 1 - 2 * way
         return inside(z - step * (hop - 1)) & inside(z + step)
 
-    def gather_start(c, hop):
+    def gather_start(c):
         for way in (0, 1):
-            @pl.when(gather_sends(way, hop))
+            @pl.when(gather_sends(way, 1))
             def _(way=way):
-                gather_copy(way, c, hop).start()
-
-    def gather_take(c, hop):
-        for way in (0, 1):
-            step = 1 - 2 * way
-
-            @pl.when(inside(z - step * hop))
-            def _(way=way, step=step):
-                block = hid.at[clamp(z - step * hop), rows_of(c), :]
-                pltpu.make_async_remote_copy(
-                    src_ref=block,
-                    dst_ref=block,
-                    send_sem=ag_send.at[way, c, hop - 1],
-                    recv_sem=ag_recv.at[way, c, hop - 1],
-                    device_id={"tensor": clamp(z + step)},
-                    device_id_type=MESH,
-                ).wait_recv()
-        if hop < parts - 1:
-            gather_start(c, hop + 1)
+                gather_copy(way, c, 1).start()
+
+    def gather_take(c, hop, way):
+        step = 1 - 2 * way
+
+        @pl.when(inside(z - step * hop))
+        def _():
+            block = hid.at[clamp(z - step * hop), rows_of(c), :]
+            pltpu.make_async_remote_copy(
+                src_ref=block,
+                dst_ref=block,
+                send_sem=ag_send.at[way, c, hop - 1],
+                recv_sem=ag_recv.at[way, c, hop - 1],
+                device_id={"tensor": clamp(z + step)},
+                device_id_type=MESH,
+            ).wait_recv()
+            if hop < parts - 1:
+                @pl.when(inside(z + step))
+                def _():
+                    gather_copy(way, c, hop + 1).start()
 
     def sum_copy(way, c, hop, source):
         step = 1 - 2 * way
         return pltpu.make_async_remote_copy(
             src_ref=source,
-            dst_ref=arrived.at[way, c, hop - 1],
+            dst_ref=arrived.at[way, hop - 1, rows_of(c), :],
             send_sem=rs_send.at[way, c, hop - 1],
             recv_sem=rs_recv.at[way, c, hop - 1],
             device_id={"tensor": clamp(z + step)},
             device_id_type=MESH,
         )
 
-    def sum_hop(c, hop):
+    def sum_hop(c, hop, way):
+        step = 1 - 2 * way
+        block = z + step * (parts - hop)
+        first = jnp.logical_not(inside(z - step))
+        own = partial.at[clamp(block), rows_of(c), :]
+
+        @pl.when(inside(block) & first)
+        def _():
+            sum_copy(way, c, hop, own).start()
+
+        if hop > 1:
+            @pl.when(inside(block) & jnp.logical_not(first))
+            def _():
+                slot = arrived.at[way, hop - 2, rows_of(c), :]
+                sum_copy(way, c, hop - 1, slot).wait_recv()
+                slot[...] = (slot[...].astype(F32) + own[...].astype(F32)).astype(BF16)
+                sum_copy(way, c, hop, slot).start()
+
+    own_counts = counts_ref[pl.ds(me, 1), :].astype(F32)
+    home_len = rows_all - jnp.sum(own_counts, axis=1, keepdims=True)
+
+    def sum_finish(c):
+        count = sizes[c]
+        sums = acc.at[pl.ds(0, count), :]
+        sums[...] = partial[z, rows_of(c), :].astype(F32)
         for way in (0, 1):
             step = 1 - 2 * way
-            block = z + step * (parts - hop)
-            first = jnp.logical_not(inside(z - step))
-
-            @pl.when(inside(block) & first)
-            def _(way=way, block=block):
-                sum_copy(way, c, hop, partial.at[c, clamp(block)]).start()
-
-            if hop > 1:
-                @pl.when(inside(block) & jnp.logical_not(first))
-                def _(way=way, block=block):
-                    slot = arrived.at[way, c, hop - 2]
-                    sum_copy(way, c, hop - 1, slot).wait_recv()
-                    slot[...] = (slot[...].astype(F32) + partial[c, clamp(block)].astype(F32)).astype(BF16)
-                    sum_copy(way, c, hop, slot).start()
-
-    own_counts = counts_ref[pl.ds(me, 1), :].astype(F32)
-    home_len = rows_all - jnp.sum(own_counts, axis=1, keepdims=True)
-
-    def sum_finish(c):
-        acc[...] = partial[c, z].astype(F32)
-        for way in (0, 1):
-            step = 1 - 2 * way
 
             @pl.when(inside(z - step))
             def _(way=way):
-                slot = arrived.at[way, c, parts - 2]
+                slot = arrived.at[way, parts - 2, rows_of(c), :]
                 sum_copy(way, c, parts - 1, slot).wait_recv()
-                acc[...] += slot[...].astype(F32)
-        total = acc[...]
+                sums[...] += slot[...].astype(F32)
+        total = sums[...]
         final[rows_of(c), :] = total.astype(BF16)
-        position = (lax.broadcasted_iota(jnp.int32, (count, 1), 0) + c * count).astype(F32)
+        position = (lax.broadcasted_iota(jnp.int32, (count, 1), 0) + starts[c]).astype(F32)
         out_ref[rows_of(c), :] = jnp.where(position < home_len, total, 0.0).astype(BF16)
 
-    def project(c):
-        @pl.loop(0, wqkv.shape[1] // TILE)
+    def halves(total, half):
+        middle = total // 2
+        return (0, middle) if half == 0 else (middle, total)
+
+    def project(c, half):
+        count = sizes[c]
+
+        @pl.loop(*halves(wqkv.shape[1] // TILE, half))
         def _(i):
             columns = pl.ds(pl.multiple_of(i * TILE, TILE), TILE)
             total = jnp.zeros((count, TILE), F32)
@@ -171,9 +237,10 @@
     doc_row = docs_ref[...].astype(F32)
 
     def attend(c):
-        seen = (c + 1) * count
+        count = sizes[c]
+        seen = starts[c] + count
         seen_rows = pl.ds(0, seen)
-        query_at = lax.broadcasted_iota(jnp.int32, (count, seen), 0) + c * count
+        query_at = lax.broadcasted_iota(jnp.int32, (count, seen), 0) + starts[c]
         key_at = lax.broadcasted_iota(jnp.int32, (count, seen), 1)
         same = doc_col[rows_of(c), :][:, :1] == doc_row[:, :seen]
         allowed = same & (key_at <= query_at)
@@ -192,52 +259,40 @@
                 total = jnp.sum(expo, axis=1, keepdims=True)
                 mix = jnp.dot(expo.astype(BF16), values, preferred_element_type=F32) / total
                 columns = pl.ds(pl.multiple_of((g * group + k) * HD, HD), HD)
-                mixed[:, columns] = mix.astype(BF16)
-
-    def project_out(c):
-        @pl.loop(0, parts * tiles_per_block)
+                mixed[pl.ds(0, count), columns] = mix.astype(BF16)
+
+    def project_out(c, half):
+        @pl.loop(*halves(parts * tiles_per_block, half))
         def _(i):
             columns = pl.ds(pl.multiple_of(i * TILE, TILE), TILE)
-            total = jnp.dot(mixed[...], wout[:, columns], preferred_element_type=F32)
+            total = jnp.dot(mixed[pl.ds(0, sizes[c]), :], wout[:, columns], preferred_element_type=F32)
             inner = pl.ds(pl.multiple_of(lax.rem(i, tiles_per_block) * TILE, TILE), TILE)
-            partial[c, lax.div(i, tiles_per_block), :, inner] = total.astype(BF16)
-
-    gather_start(0, 1)
+            partial[lax.div(i, tiles_per_block), rows_of(c), inner] = total.astype(BF16)
+
     for k in range(rows_all // HD):
         doc_col[pl.ds(k * HD, HD), :] = jnp.broadcast_to(doc_row[:, k * HD:(k + 1) * HD], (HD, HD)).T
-    for hop in range(1, parts - 1):
-        gather_take(0, hop)
-    if chunks > 1:
-        gather_start(1, 1)
-    load_own.wait()
-    for c in range(chunks):
-        gather_take(c, parts - 1)
-        if c == 0:
-            for load in loads_qkv:
-                load.wait()
-        project(c)
-        if c + 1 < chunks:
-            for hop in range(1, parts - 2):
-                gather_take(c + 1, hop)
-        if c > 0:
-            for hop in range(2, parts - 1):
-                sum_hop(c - 1, hop)
-        attend(c)
-        if c == 0:
-            load_out.wait()
-        project_out(c)
-        if c + 1 < chunks:
-            gather_take(c + 1, parts - 2)
-            if c + 2 < chunks:
-                gather_start(c + 2, 1)
-        if c > 0:
-            sum_hop(c - 1, parts - 1)
-        sum_hop(c, 1)
-        if c > 0:
-            sum_finish(c - 1)
-    for hop in range(2, parts):
-        sum_hop(chunks - 1, hop)
-    sum_finish(chunks - 1)
+    for step in order:
+        kind, c = step[0], step[1]
+        if kind == "send":
+            gather_start(c)
+        elif kind == "take":
+            gather_take(c, step[2], step[3])
+        elif kind == "project":
+            if c == 0 and step[2] == 0:
+                load_own.wait()
+                for load in loads_qkv:
+                    load.wait()
+            project(c, step[2])
+        elif kind == "attend":
+            attend(c)
+        elif kind == "out":
+            if c == 0 and step[2] == 0:
+                load_out.wait()
+            project_out(c, step[2])
+        elif kind == "sum":
+            sum_hop(c, step[2], step[3])
+        else:
+            sum_finish(c)
 
     moved = peers * SLOT
     at = lax.broadcasted_iota(jnp.int32, (moved, peers), 0)
@@ -280,7 +335,7 @@
             @pl.when(inside(z + (1 - 2 * way) * (parts - hop)))
             def _(way=way, hop=hop):
                 for c in range(chunks):
-                    sum_copy(way, c, hop, arrived.at[way, c, hop - 1]).wait_send()
+                    sum_copy(way, c, hop, arrived.at[way, hop - 1, rows_of(c), :]).wait_send()
 
     @pl.loop(1, peers)
     def _(i):
@@ -295,15 +350,16 @@
     rows, width = hidden.shape
     q_heads = w_query.shape[1] // HD
     kv_heads = w_key.shape[1] // HD
-    chunks = CHUNKS
-    count = rows // chunks
+    sizes = SIZES
+    order = ORDER if parts == 4 else plain_order(parts, len(sizes))
+    chunks, most = len(sizes), max(sizes)
     features = w_query.shape[0]
     moved = peers * SLOT
     anywhere = pl.BlockSpec(memory_space=pl.ANY)
     in_vmem = pl.BlockSpec(memory_space=pltpu.VMEM)
     hops = parts - 1
     return pl.pallas_call(
-        functools.partial(layer_kernel, peers, parts, chunks, q_heads, kv_heads),
+        functools.partial(layer_kernel, peers, parts, sizes, order, q_heads, kv_heads),
         out_shape=jax.ShapeDtypeStruct((rows + moved, width), BF16),
         in_specs=[anywhere] * 5 + [in_vmem] * 2,
         out_specs=in_vmem,
@@ -312,10 +368,10 @@
             pltpu.VMEM(w_out.shape, BF16),
             pltpu.VMEM((parts, rows, width), BF16),
             pltpu.VMEM((q_heads + 2 * kv_heads, rows, HD), BF16),
-            pltpu.VMEM((count, q_heads * HD), BF16),
-            pltpu.VMEM((chunks, parts, count, width), BF16),
-            pltpu.VMEM((2, chunks, hops, count, width), BF16),
-            pltpu.VMEM((count, width), F32),
+            pltpu.VMEM((most, q_heads * HD), BF16),
+            pltpu.VMEM((parts, rows, width), BF16),
+            pltpu.VMEM((2, hops, rows, width), BF16),
+            pltpu.VMEM((most, width), F32),
             pltpu.VMEM((rows, width), BF16),
             pltpu.VMEM((moved, width), BF16),
             pltpu.VMEM((moved, width), BF16),

time: 134 us -> 128 us (0.955)
  Pallas kernels: 131 us -> 125 us
    pallas_call x1, Pallas kernels: 131 us -> 125 us  [on_device(): pl.pallas_call(functools.partial(layer_kernel, peers, parts, sizes, order...]
where the time goes in v2:
time: 128 us
  Pallas kernels  125 us (98%)
  local copies, waits for them, and re-layouts  2.47 us (2%)
    pallas_call x1, Pallas kernels, on_device(): pl.pallas_call(functools.partial(layer_kernel, peers, parts, sizes, order...  125 us

profile of v2, /device:TPU:0, one launch (start us, length us, event | category | flops | bytes accessed | tf_op | source)
XLA Modules:
  0.0 127.6 jit_solution(11593894914239529620)
XLA Ops:
  0.0 125.1 %layer.1 = bf16[640,1024]{1,0:T(8,128)(2,1)} custom-call(bf16[512,1024]{1,0:T(8,128)(2,1)} %hidden_ref.1, bf16[4096,1024]{1,0:T(8,128)(2,1)} %wq_ref.1, bf16[4096,256]{1,0:T(8,128)(2,1)} %wk_ref.1, bf16[4096,256]{1,0:T(8,128)(2,1)} %wv_ref.1, bf16[1024,4096]{1,0:T(8,128)(2,1)} %wo_ref.1, s32[1,512]{1,0:T(1,128)} %bitcast.1, s32[8,8]{1,0:T(8,128)} %counts_ref.1), custom_call_target="tpu_custom_call" | custom-call | tf_op jit(solution)/shard_map/layer/pallas_call | solution.py:361
  125.1 2.5 %copy.9 = bf16[640,1024]{1,0:T(8,128)(2,1)} copy(bf16[640,1024]{1,0:T(8,128)(2,1)} %layer.1) | data formatting | bytes 2621440
